TPU v7x, 768 devices: a whole 4x8x12 slice. The times are simulated.
768 devices in a mesh: rep: 16 (over x_lo, y), shard: 48 (over x_hi, z, core).
Axes of the slice: x: 4 (x_hi: 2, x_lo: 2; x = x_hi * 2 + x_lo), y: 8, z: 12, core: 2. Of those that a mesh axis runs over, the one named last changes fastest.
Arguments:
- queries: bfloat16 [589824, 512], P(('rep', 'shard')), may hold values from -1.5909903 to 1.5909903
- target_ids: int32 [36864, 16], P(('rep', 'shard')), may hold values from 0 to 511
- negative_ids: int32 [36864, 16], P(('rep', 'shard')), may hold values from 0 to 511
- table_rows: float32 [24576, 512], P('shard'), may hold values from -1.5909903 to 1.5909903
- first_moment: float32 [24576, 512], P('shard'), may hold values from -0.5 to 0.5
- second_moment: float32 [24576], P('shard'), may hold values from 0.001 to 0.1
Outputs:
- new_rows: float32 [24576, 512], P('shard')
- new_first: float32 [24576, 512], P('shard')
- new_second: float32 [24576], P('shard')
- grad_queries: float32 [589824, 512], P(('rep', 'shard'))
All inputs are finite; a program needn't handle non-finite values.
Results may differ from a plain program's by a relative error of at most 0.0013.
The roundings to bfloat16 on the way count: a program that leaves them out, or rounds other values in their place, can miss the bound.
Values may be sent and summed in bfloat16 or wider, within the bound.
A program may use at most 64 MiB of HBM per device.

v0:
```python
import jax
import jax.numpy as jnp
from jax import lax
from jax.sharding import PartitionSpec as P

SCALE = 72.0


def unit_rows(values):
    norm = jnp.sqrt(jnp.sum(values * values, axis=-1, keepdims=True) + 1e-06)
    return (values / norm, norm)


def project_back(grad, unit, norm):
    return (grad - unit * jnp.sum(unit * grad, axis=-1, keepdims=True)) / norm


def prepare(arrived, query_bf):
    width = arrived.shape[-1]
    cand_unit, cand_norm = unit_rows(arrived.reshape(-1, width).astype(jnp.float32))
    cand_bf = cand_unit.astype(jnp.bfloat16)
    weights = jnp.exp(jnp.dot(query_bf, cand_bf.T, preferred_element_type=jnp.float32) * SCALE)
    return (cand_unit, cand_norm, cand_bf, weights)


def adam_rows(rows, first, second, grad):
    new_first = 0.9 * first + 0.1 * grad
    new_second = 0.999 * second + 0.001 * jnp.mean(grad * grad, axis=-1)
    new_rows = rows - 0.01 * new_first / (jnp.sqrt(new_second)[:, None] + 1e-08)
    return (new_rows, new_first, new_second)


def per_device(queries, target_ids, negative_ids, table_rows, first_moment, second_moment):
    width = queries.shape[1]
    owners, per_target = target_ids.shape
    per_negative = negative_ids.shape[1]
    outgoing = table_rows.astype(jnp.bfloat16)
    asked_targets, asked_negatives = (
        lax.all_to_all(target_ids, "shard", split_axis=0, concat_axis=0, tiled=True),
        lax.all_to_all(negative_ids, "shard", split_axis=0, concat_axis=0, tiled=True),
    )
    send_targets = outgoing[asked_targets]
    send_negatives = outgoing[asked_negatives]
    query_unit, query_norm = unit_rows(queries.astype(jnp.float32))
    query_bf = query_unit.astype(jnp.bfloat16)
    got_targets, got_negatives = (
        lax.all_to_all(send_targets, "shard", split_axis=0, concat_axis=0, tiled=True),
        lax.all_to_all(send_negatives, "shard", split_axis=0, concat_axis=0, tiled=True),
    )
    target_unit, target_norm, target_bf, weights_t = prepare(got_targets, query_bf)
    negative_unit, negative_norm, negative_bf, weights_n = prepare(got_negatives, query_bf)
    total = jnp.sum(weights_t, axis=1, keepdims=True) + jnp.sum(weights_n, axis=1, keepdims=True)
    rows_idx = lax.broadcasted_iota(jnp.int32, weights_t.shape, 0)
    cols_idx = lax.broadcasted_iota(jnp.int32, weights_t.shape, 1)
    labels = jnp.where(rows_idx == cols_idx, 1.0, 0.0).astype(jnp.float32)
    coef_t = (weights_t / total - labels).astype(jnp.bfloat16)
    coef_n = (weights_n / total).astype(jnp.bfloat16)
    query_grad = (
        jnp.dot(coef_t, target_bf, preferred_element_type=jnp.float32)
        + jnp.dot(coef_n, negative_bf, preferred_element_type=jnp.float32)
    ) * SCALE
    grad_queries = project_back(query_grad, query_unit, query_norm)
    target_grad = jnp.dot(coef_t.T, query_bf, preferred_element_type=jnp.float32) * SCALE
    negative_grad = jnp.dot(coef_n.T, query_bf, preferred_element_type=jnp.float32) * SCALE
    target_back = (
        project_back(target_grad, target_unit, target_norm)
        .astype(jnp.bfloat16)
        .reshape(owners, per_target, width)
    )
    negative_back = (
        project_back(negative_grad, negative_unit, negative_norm)
        .astype(jnp.bfloat16)
        .reshape(owners, per_negative, width)
    )
    came_targets, came_negatives = (
        lax.all_to_all(target_back, "shard", split_axis=0, concat_axis=0, tiled=True),
        lax.all_to_all(negative_back, "shard", split_axis=0, concat_axis=0, tiled=True),
    )
    local = jnp.zeros((table_rows.shape[0], width), jnp.float32)
    local = local.at[asked_targets.reshape(-1)].add(
        came_targets.reshape(-1, width).astype(jnp.float32)
    )
    local = local.at[asked_negatives.reshape(-1)].add(
        came_negatives.reshape(-1, width).astype(jnp.float32)
    )
    grad = lax.psum(local, "rep")
    new_rows, new_first, new_second = adam_rows(table_rows, first_moment, second_moment, grad)
    return (new_rows, new_first, new_second, grad_queries)


def solution(mesh):
    return jax.shard_map(
        per_device,
        mesh=mesh,
        in_specs=(
            P(("rep", "shard"), None),
            P(("rep", "shard"), None),
            P(("rep", "shard"), None),
            P("shard", None),
            P("shard", None),
            P("shard"),
        ),
        out_specs=(P("shard", None), P("shard", None), P("shard"), P(("rep", "shard"), None)),
        check_vma=False,
    )
```

profile of v0, /device:TPU:6, one launch (start us, length us, event | category | flops | bytes accessed | tf_op | source)
XLA Modules:
  0.0 378.6 jit_solution(499749026572180446)
XLA Ops:
  7.2 1.4 copy.19
  8.6 18.5 %all-to-all-start.2 = ((s32[48,1,16]{2,1,0:T(1,128)}), s32[48,1,16]{2,1,0:T(1,128)S(1)}, u32[]{:S(2)}, u32[]{:S(2)}) async-start(s32[48,1,16]{2,1,0:T(1,128)} %bitcast.4), calls=%async_computation.2 | async-start | bytes 49152 | tf_op jit(solution)/shard_map/all_to_all | solution.py:40
  27.1 1.3 convert_element_type.59
  29.1 7.5 %all-to-all-done.2 = s32[48,1,16]{2,1,0:T(1,128)S(1)} async-done(((s32[48,1,16]{2,1,0:T(1,128)}), s32[48,1,16]{2,1,0:T(1,128)S(1)}, u32[]{:S(2)}, u32[]{:S(2)}) %all-to-all-start.2) | async-done | bytes 3104 | tf_op jit(solution)/shard_map/all_to_all | solution.py:40
  36.6 7.2 %all-to-all-start = ((s32[48,1,16]{2,1,0:T(1,128)}), s32[48,1,16]{2,1,0:T(1,128)S(1)}, u32[]{:S(2)}, u32[]{:S(2)}) async-start(s32[48,1,16]{2,1,0:T(1,128)} %bitcast), calls=%async_computation | async-start | bytes 49152 | tf_op jit(solution)/shard_map/all_to_all | solution.py:39
  43.8 3.3 gather_fusion.1
  47.2 6.1 %all-to-all-done = s32[48,1,16]{2,1,0:T(1,128)S(1)} async-done(((s32[48,1,16]{2,1,0:T(1,128)}), s32[48,1,16]{2,1,0:T(1,128)S(1)}, u32[]{:S(2)}, u32[]{:S(2)}) %all-to-all-start) | async-done | bytes 3104 | tf_op jit(solution)/shard_map/all_to_all | solution.py:39
  53.2 7.2 %all-to-all-start.3 = ((bf16[48,16,512]{2,1,0:T(8,128)(2,1)}), bf16[48,16,512]{2,1,0:T(8,128)(2,1)S(1)}, u32[]{:S(2)}, u32[]{:S(2)}) async-start(bf16[48,16,512]{2,1,0:T(8,128)(2,1)} %bitcast.6), calls=%async_computation.3 | async-start | bytes 1572864 | tf_op jit(solution)/shard_map/all_to_all | solution.py:48
  60.6 3.3 gather_fusion
  63.9 25.7 %all-to-all-done.3 = bf16[48,16,512]{2,1,0:T(8,128)(2,1)S(1)} async-done(((bf16[48,16,512]{2,1,0:T(8,128)(2,1)}), bf16[48,16,512]{2,1,0:T(8,128)(2,1)S(1)}, u32[]{:S(2)}, u32[]{:S(2)}) %all-to-all-start.3) | async-done | bytes 786464 | tf_op jit(solution)/shard_map/all_to_all | solution.py:48
  89.6 10.1 %all-to-all-start.1 = ((bf16[48,16,512]{2,1,0:T(8,128)(2,1)}), bf16[48,16,512]{2,1,0:T(8,128)(2,1)S(1)}, u32[]{:S(2)}, u32[]{:S(2)}) async-start(bf16[48,16,512]{2,1,0:T(8,128)(2,1)} %bitcast.2), calls=%async_computation.1 | async-start | bytes 1572864 | tf_op jit(solution)/shard_map/all_to_all | solution.py:47
  100.3 28.6 %all-to-all-done.1 = bf16[48,16,512]{2,1,0:T(8,128)(2,1)S(1)} async-done(((bf16[48,16,512]{2,1,0:T(8,128)(2,1)}), bf16[48,16,512]{2,1,0:T(8,128)(2,1)S(1)}, u32[]{:S(2)}, u32[]{:S(2)}) %all-to-all-start.1) | async-done | bytes 786464 | tf_op jit(solution)/shard_map/all_to_all | solution.py:47
  129.4 2.3 fusion.1
  132.0 0.9 fusion
  132.9 1.0 multiply_reduce_fusion.2
  134.3 1.3 divide_convert_fusion.2
  135.6 10.1 %all-to-all-start.4 = ((bf16[48,16,512]{2,1,0:T(8,128)(2,1)}), bf16[48,16,512]{2,1,0:T(8,128)(2,1)S(1)}, u32[]{:S(2)}, u32[]{:S(2)}) async-start(bf16[48,16,512]{2,1,0:T(8,128)(2,1)} %bitcast.8), calls=%async_computation.4 | async-start | bytes 1572864 | tf_op jit(solution)/shard_map/all_to_all | solution.py:76
  145.7 2.7 multiply_reduce_fusion.1
  148.3 1.3 divide_convert_fusion.1
  149.6 25.2 %all-to-all-done.4 = bf16[48,16,512]{2,1,0:T(8,128)(2,1)S(1)} async-done(((bf16[48,16,512]{2,1,0:T(8,128)(2,1)}), bf16[48,16,512]{2,1,0:T(8,128)(2,1)S(1)}, u32[]{:S(2)}, u32[]{:S(2)}) %all-to-all-start.4) | async-done | bytes 786464 | tf_op jit(solution)/shard_map/all_to_all | solution.py:76
  174.8 10.1 %all-to-all-start.5 = ((bf16[48,16,512]{2,1,0:T(8,128)(2,1)}), bf16[48,16,512]{2,1,0:T(8,128)(2,1)S(1)}, u32[]{:S(2)}, u32[]{:S(2)}) async-start(bf16[48,16,512]{2,1,0:T(8,128)(2,1)} %bitcast.10), calls=%async_computation.5 | async-start | bytes 1572864 | tf_op jit(solution)/shard_map/all_to_all | solution.py:77
  186.2 0.7 reduce.13
  187.1 3.6 fusion.11
  190.7 7.1 %scatter_custom_fusion = f32[512,512]{1,0:T(8,128)S(1)} fusion(s32[768]{0:T(1024)S(1)} %fusion.15, bf16[768,512]{1,0:T(8,128)(2,1)S(1)} %bitcast.33, f32[]{:T(128)} %constant.13.clone.1), kind=kCustom, calls=%fused_computation.16 | custom fusion | flops 786432 | bytes 1835012 | tf_op jit(solution)/shard_map/scatter-add | solution.py:80
  197.8 16.2 %all-to-all-done.5 = bf16[48,16,512]{2,1,0:T(8,128)(2,1)S(1)} async-done(((bf16[48,16,512]{2,1,0:T(8,128)(2,1)}), bf16[48,16,512]{2,1,0:T(8,128)(2,1)S(1)}, u32[]{:S(2)}, u32[]{:S(2)}) %all-to-all-start.5) | async-done | bytes 786464 | tf_op jit(solution)/shard_map/all_to_all | solution.py:77
  214.0 7.2 %scatter_custom_fusion.1 = f32[512,512]{1,0:T(8,128)S(1)} fusion(f32[512,512]{1,0:T(8,128)S(1)} %scatter_custom_fusion, s32[768]{0:T(1024)S(1)} %fusion.16, bf16[768,512]{1,0:T(8,128)(2,1)S(1)} %bitcast.32), kind=kCustom, calls=%fused_computation.14 | custom fusion | flops 786432 | bytes 1835008 | tf_op jit(solution)/shard_map/scatter-add | solution.py:83
  221.3 1.0 copy-done.2
  222.3 3.1 multiply_reduce_fusion
  225.4 1.5 subtract_divide_fusion
  226.9 141.1 %all-reduce.2.cloned.1.call-done = f32[512,512]{1,0:T(8,128)} async-done(((f32[512,512]{1,0:T(8,128)}), f32[512,512]{1,0:T(8,128)}) %all-reduce.2.cloned.1.call-update) | async-done | bytes 1048592 | tf_op jit(solution)/shard_map/psum | solution.py:86
  368.1 1.5 multiply_reduce_fusion.5
  370.1 1.6 divide_subtract_fusion
  (46 shorter events, 4.6 us)
Async XLA Ops:
  7.2 21.2 %copy-start.7 = (s32[48,16]{0,1:T(8,128)S(1)}, s32[48,16]{0,1:T(8,128)}, u32[]{:S(2)}) copy-start(s32[48,16]{0,1:T(8,128)} %param.7) | copy-start | bytes 9220
  8.6 28.0 %all-to-all-start.2 = ((s32[48,1,16]{2,1,0:T(1,128)}), s32[48,1,16]{2,1,0:T(1,128)S(1)}, u32[]{:S(2)}, u32[]{:S(2)}) async-start(s32[48,1,16]{2,1,0:T(1,128)} %bitcast.4), calls=%async_computation.2 | async-start | bytes 49152 | tf_op jit(solution)/shard_map/all_to_all | solution.py:40
  36.6 16.7 %all-to-all-start = ((s32[48,1,16]{2,1,0:T(1,128)}), s32[48,1,16]{2,1,0:T(1,128)S(1)}, u32[]{:S(2)}, u32[]{:S(2)}) async-start(s32[48,1,16]{2,1,0:T(1,128)} %bitcast), calls=%async_computation | async-start | bytes 49152 | tf_op jit(solution)/shard_map/all_to_all | solution.py:39
  53.2 36.4 %all-to-all-start.3 = ((bf16[48,16,512]{2,1,0:T(8,128)(2,1)}), bf16[48,16,512]{2,1,0:T(8,128)(2,1)S(1)}, u32[]{:S(2)}, u32[]{:S(2)}) async-start(bf16[48,16,512]{2,1,0:T(8,128)(2,1)} %bitcast.6), calls=%async_computation.3 | async-start | bytes 1572864 | tf_op jit(solution)/shard_map/all_to_all | solution.py:48
  63.9 35.8 %copy-start.3 = (bf16[768,512]{1,0:T(8,128)(2,1)S(1)}, bf16[768,512]{1,0:T(8,128)(2,1)}, u32[]{:S(2)}) copy-start(bf16[768,512]{1,0:T(8,128)(2,1)} %param.6) | copy-start | bytes 2359300
  89.6 39.2 %all-to-all-start.1 = ((bf16[48,16,512]{2,1,0:T(8,128)(2,1)}), bf16[48,16,512]{2,1,0:T(8,128)(2,1)S(1)}, u32[]{:S(2)}, u32[]{:S(2)}) async-start(bf16[48,16,512]{2,1,0:T(8,128)(2,1)} %bitcast.2), calls=%async_computation.1 | async-start | bytes 1572864 | tf_op jit(solution)/shard_map/all_to_all | solution.py:47
  129.4 2.3 copy-start.5
  132.9 1.4 copy-start.9
  135.6 39.2 %all-to-all-start.4 = ((bf16[48,16,512]{2,1,0:T(8,128)(2,1)}), bf16[48,16,512]{2,1,0:T(8,128)(2,1)S(1)}, u32[]{:S(2)}, u32[]{:S(2)}) async-start(bf16[48,16,512]{2,1,0:T(8,128)(2,1)} %bitcast.8), calls=%async_computation.4 | async-start | bytes 1572864 | tf_op jit(solution)/shard_map/all_to_all | solution.py:76
  174.8 39.2 %all-to-all-start.5 = ((bf16[48,16,512]{2,1,0:T(8,128)(2,1)}), bf16[48,16,512]{2,1,0:T(8,128)(2,1)S(1)}, u32[]{:S(2)}, u32[]{:S(2)}) async-start(bf16[48,16,512]{2,1,0:T(8,128)(2,1)} %bitcast.10), calls=%async_computation.5 | async-start | bytes 1572864 | tf_op jit(solution)/shard_map/all_to_all | solution.py:77
  184.9 183.2 %all-reduce.2.cloned.1.call-start = ((), (), s32[]{:S(2)}) async-start(), calls=%async_computation.6 | async-start | bytes 2097152 | tf_op jit(solution)/shard_map/psum | solution.py:86
  197.8 24.4 %copy-start.6 = (bf16[768,512]{1,0:T(8,128)(2,1)S(1)}, bf16[768,512]{1,0:T(8,128)(2,1)}, u32[]{:S(2)}) copy-start(bf16[768,512]{1,0:T(8,128)(2,1)} %copy-done.5) | copy-start | bytes 2359300
  221.3 1.0 copy-start.2
  225.4 144.2 %copy-start.8 = (f32[512]{0:T(512)S(1)}, f32[512]{0:T(512)}, u32[]{:S(2)}) copy-start(f32[512]{0:T(512)} %param.11) | copy-start | bytes 6148
  225.4 144.7 %copy-start = (f32[512,512]{1,0:T(8,128)S(1)}, f32[512,512]{1,0:T(8,128)}, u32[]{:S(2)}) copy-start(f32[512,512]{1,0:T(8,128)} %param.9) | copy-start | bytes 3145732
  225.4 144.7 %copy-start.4 = (f32[512,512]{1,0:T(8,128)S(1)}, f32[512,512]{1,0:T(8,128)}, u32[]{:S(2)}) copy-start(f32[512,512]{1,0:T(8,128)} %param.10) | copy-start | bytes 3145732
  368.1 2.1 copy-start.1
Sparse Core Ops, SparseCore 0:
  222.4 145.6 all-reduce.1
where the time goes:
time: 380 us; the launch traced here: 379 us
  waiting for transfers between devices  250 us (66%)
  starting transfers between devices  63.2 us (17%)
  other arithmetic  26 us (7%)
  between operations  14.3 us (4%)
  matrix products  13.6 us (4%)
  local copies, waits for them, and re-layouts  11.1 us (3%)
    psum x1, waiting for transfers between devices, per_device(): grad = lax.psum(local, 'rep')  141 us
    all_to_all x1, waiting for transfers between devices, per_device(): lax.all_to_all(send_targets, 'shard', split_axis=0, concat_axis=0, tiled=...  28.6 us
    all_to_all x1, waiting for transfers between devices, per_device(): lax.all_to_all(send_negatives, 'shard', split_axis=0, concat_axis=0, tile...  25.7 us
    all_to_all x1, waiting for transfers between devices, per_device(): lax.all_to_all(target_back, 'shard', split_axis=0, concat_axis=0, tiled=T...  25.2 us
    all_to_all x1, starting transfers between devices, per_device(): lax.all_to_all(negative_ids, 'shard', split_axis=0, concat_axis=0, tiled=...  18.5 us
    all_to_all x1, waiting for transfers between devices, per_device(): lax.all_to_all(negative_back, 'shard', split_axis=0, concat_axis=0, tiled...  16.2 us
    all_to_all x1, starting transfers between devices, per_device(): lax.all_to_all(target_back, 'shard', split_axis=0, concat_axis=0, tiled=T...  10.1 us
    all_to_all x1, starting transfers between devices, per_device(): lax.all_to_all(send_targets, 'shard', split_axis=0, concat_axis=0, tiled=...  10.1 us
  transfers between devices with their start and end apart: 7, of which 7 were waited for; matrix products, arithmetic and copies ran while one was open for 8% of the time, Pallas kernels for 0%

commit v1 on v0

v1 whole, which is shorter than its diff:
```python
import functools

import jax
import jax.numpy as jnp
from jax import lax
from jax.experimental import pallas as pl
from jax.experimental.pallas import tpu as pltpu
from jax.sharding import PartitionSpec as P

SCALE = 72.0
EPS = 1e-06
CHUNKS = 2
BAND = 8
F32 = jnp.float32
BF16 = jnp.bfloat16
NT = (((1,), (1,)), ((), ()))
TN = (((0,), (0,)), ((), ()))


def iota(shape, axis):
    return lax.broadcasted_iota(jnp.int32, shape, axis)


def push(src, dst, send, recv, axis, peer):
    return pltpu.make_async_remote_copy(
        src_ref=src,
        dst_ref=dst,
        send_sem=send,
        recv_sem=recv,
        device_id={axis: peer},
        device_id_type=pl.DeviceIdType.MESH,
    )


def kernel(
    reps,
    shards,
    per_target,
    ids_ref,
    q_ref,
    table_ref,
    gq_ref,
    grad_ref,
    ids_in,
    table_bf,
    onehot_t,
    outgoing,
    arrived,
    query_unit,
    query_norm,
    query_bf,
    cand_unit,
    cand_norm,
    cand_bf,
    weights,
    coef,
    back,
    came,
    local,
    parts,
    gathered,
    ids_send,
    ids_recv,
    rows_send,
    rows_recv,
    back_send,
    back_recv,
    part_send,
    part_recv,
    full_send,
    full_recv,
    own_sem,
):
    me = lax.axis_index("shard")
    rep = lax.axis_index("rep")
    per_peer = outgoing.shape[1]
    uniq, width = table_bf.shape
    tokens = query_bf.shape[0]
    bands = shards // BAND
    band_rows = BAND * per_peer
    lanes = 128
    packs = band_rows // lanes
    per_pack = lanes // per_peer
    span = width // CHUNKS
    slice_rows = uniq // reps
    my_band = me // BAND

    def to_shards(body):
        def step(k, carry):
            body(lax.rem(me + k, shards))
            return carry

        lax.fori_loop(1, shards, step, 0)

    def to_reps(body):
        def step(k, carry):
            body(lax.rem(rep + k, reps))
            return carry

        lax.fori_loop(1, reps, step, 0)

    barrier = pltpu.get_barrier_semaphore()
    to_shards(
        lambda p: pl.semaphore_signal(
            barrier, inc=1, device_id={"shard": p}, device_id_type=pl.DeviceIdType.MESH
        )
    )
    to_reps(
        lambda p: pl.semaphore_signal(
            barrier, inc=1, device_id={"rep": p}, device_id_type=pl.DeviceIdType.MESH
        )
    )
    table_bf[...] = table_ref[...].astype(BF16)
    pl.semaphore_wait(barrier, shards + reps - 2)

    to_shards(
        lambda p: push(ids_ref.at[p], ids_in.at[me], ids_send, ids_recv, "shard", p).start()
    )
    ids_in[me] = ids_ref[me]

    values = q_ref[...].astype(F32)
    norm = jnp.sqrt(jnp.sum(values * values, axis=-1, keepdims=True) + EPS)
    unit = values / norm
    query_norm[...] = norm
    query_unit[...] = unit
    query_bf[...] = unit.astype(BF16)

    others = pl.ds(0, shards - 1)
    push(ids_in.at[others], ids_in.at[others], ids_send, ids_recv, "shard", me).wait()

    def gather(i, carry):
        band = lax.rem(my_band + i, bands)
        first = band * BAND
        which = iota((1, lanes), 1) // per_peer
        flat = []
        tall = []
        for pack in range(packs):
            row = ids_in[first + pack * per_pack]
            for j in range(1, per_pack):
                row = jnp.where(which == j, ids_in[first + pack * per_pack + j], row)
            flat.append(row)
            tall.append(jnp.transpose(jnp.broadcast_to(row, (lanes, lanes))))
        row = jnp.concatenate(flat, axis=1)
        onehot_t[band] = jnp.where(iota((uniq, band_rows), 0) == row, 1.0, 0.0).astype(BF16)
        column = jnp.concatenate(tall, axis=0)
        column = jnp.concatenate([column] * (uniq // lanes), axis=1)
        onehot = jnp.where(iota((band_rows, uniq), 1) == column, 1.0, 0.0).astype(BF16)
        rows = jnp.dot(onehot, table_bf[...], preferred_element_type=F32).astype(BF16)
        outgoing[pl.ds(first, BAND)] = rows.reshape(BAND, per_peer, width)
        for j in range(BAND):
            peer = first + j

            @pl.when(peer != me)
            def _():
                push(
                    outgoing.at[peer], arrived.at[me], rows_send, rows_recv.at[my_band], "shard", peer
                ).start()

            @pl.when(peer == me)
            def _():
                pltpu.make_async_copy(
                    outgoing.at[peer], arrived.at[me], rows_recv.at[my_band]
                ).start()

        return carry

    lax.fori_loop(0, bands, gather, 0)

    def score(i, total):
        band = lax.rem(my_band + i, bands)
        peers = pl.ds(band * BAND, BAND)
        push(
            arrived.at[peers], arrived.at[peers], rows_send, rows_recv.at[band], "shard", me
        ).wait_recv()
        values = arrived[peers].reshape(band_rows, width).astype(F32)
        norm = jnp.sqrt(jnp.sum(values * values, axis=-1, keepdims=True) + EPS)
        unit = values / norm
        unit_bf = unit.astype(BF16)
        cand_norm[band] = norm
        cand_unit[band] = unit
        cand_bf[band] = unit_bf
        scores = lax.dot_general(unit_bf, query_bf[...], NT, preferred_element_type=F32) * SCALE
        weight = jnp.exp(scores)
        weights[band] = weight
        return total + jnp.sum(weight, axis=0, keepdims=True)

    total = lax.fori_loop(0, bands, score, jnp.zeros((1, tokens), F32))
    share = 1.0 / total

    def send_back(chunk, peer):
        push(
            back.at[chunk, peer],
            came.at[chunk, me],
            back_send,
            back_recv.at[chunk],
            "shard",
            peer,
        ).start()

    def row_grads(i, carry):
        band = lax.rem(my_band + i, bands)
        first = band * BAND
        place = iota((band_rows, 1), 0) + band * band_rows
        slot = lax.rem(place, per_peer)
        target = jnp.where(slot < per_target, place // per_peer * per_target + slot, -1)
        label = jnp.where(iota((band_rows, tokens), 1) == target, 1.0, 0.0)
        coef_band = (weights[band] * share - label).astype(BF16)
        coef[band] = coef_band
        grad = jnp.dot(coef_band, query_bf[...], preferred_element_type=F32) * SCALE
        unit = cand_unit[band]
        grad = (grad - unit * jnp.sum(unit * grad, axis=-1, keepdims=True)) / cand_norm[band]
        grad = grad.astype(BF16)
        for chunk in range(CHUNKS):
            back[chunk, pl.ds(first, BAND)] = grad[:, chunk * span : (chunk + 1) * span].reshape(
                BAND, per_peer, span
            )
        for j in range(BAND):
            peer = first + j

            @pl.when(peer != me)
            def _():
                send_back(0, peer)

        return carry

    lax.fori_loop(0, bands, row_grads, 0)
    for chunk in range(1, CHUNKS):
        to_shards(functools.partial(send_back, chunk))
    for chunk in range(CHUNKS):
        pltpu.make_async_copy(back.at[chunk, me], came.at[chunk, me], back_recv.at[chunk]).start()

    tile = 256 if tokens % 256 == 0 else 128

    def query_grads(i, carry):
        at = pl.ds(pl.multiple_of(i * tile, tile), tile)
        grad = jnp.zeros((tile, width), F32)
        for band in range(bands):
            grad += lax.dot_general(
                coef[band, :, at], cand_bf[band], TN, preferred_element_type=F32
            )
        grad = grad * SCALE
        unit = query_unit[at]
        gq_ref[at] = (grad - unit * jnp.sum(unit * grad, axis=-1, keepdims=True)) / query_norm[at]
        return carry

    lax.fori_loop(0, tokens // tile, query_grads, 0)

    def reduce_chunk(chunk):
        push(
            came.at[chunk], came.at[chunk], back_send, back_recv.at[chunk], "shard", me
        ).wait_recv()
        for half in range(2):
            rows = pl.ds(half * (uniq // 2), uniq // 2)
            grad = jnp.zeros((uniq // 2, span), F32)
            for band in range(bands):
                grad += jnp.dot(
                    onehot_t[band, rows, :],
                    came[chunk, pl.ds(band * BAND, BAND)].reshape(band_rows, span),
                    preferred_element_type=F32,
                )
            local[chunk, pl.ds(half * (reps // 2), reps // 2)] = grad.reshape(
                reps // 2, slice_rows, span
            )
        to_reps(
            lambda p: push(
                local.at[chunk, p], parts.at[chunk, rep], part_send, part_recv.at[chunk], "rep", p
            ).start()
        )

    def share_chunk(chunk):
        other = pl.ds(0, reps - 1)
        push(
            parts.at[chunk, other],
            parts.at[chunk, other],
            part_send,
            part_recv.at[chunk],
            "rep",
            rep,
        ).wait_recv()
        parts[chunk, rep] = local[chunk, rep]
        gathered[chunk, rep] = jnp.sum(parts[chunk], axis=0)
        to_reps(
            lambda p: push(
                gathered.at[chunk, rep],
                gathered.at[chunk, rep],
                full_send,
                full_recv.at[chunk],
                "rep",
                p,
            ).start()
        )

    def finish_chunk(chunk):
        other = pl.ds(0, reps - 1)
        push(
            gathered.at[chunk, other],
            gathered.at[chunk, other],
            full_send,
            full_recv.at[chunk],
            "rep",
            rep,
        ).wait_recv()
        grad_ref[:, chunk * span : (chunk + 1) * span] = gathered[chunk].reshape(uniq, span)

    for chunk in range(CHUNKS):
        reduce_chunk(chunk)
        share_chunk(chunk)
    for chunk in range(CHUNKS):
        finish_chunk(chunk)

    other_rows = pl.ds(0, shards - 1)
    push(
        outgoing.at[other_rows], outgoing.at[other_rows], rows_send, ids_recv, "shard", me
    ).wait_send()
    for chunk in range(CHUNKS):
        other = pl.ds(0, shards - 1)
        push(
            back.at[chunk, other], back.at[chunk, other], back_send, ids_recv, "shard", me
        ).wait_send()
        other = pl.ds(0, reps - 1)
        push(
            local.at[chunk, other], local.at[chunk, other], part_send, ids_recv, "rep", rep
        ).wait_send()
        push(
            gathered.at[chunk, other], gathered.at[chunk, other], full_send, ids_recv, "rep", rep
        ).wait_send()


def adam_rows(rows, first, second, grad):
    new_first = 0.9 * first + 0.1 * grad
    new_second = 0.999 * second + 0.001 * jnp.mean(grad * grad, axis=-1)
    new_rows = rows - 0.01 * new_first / (jnp.sqrt(new_second)[:, None] + 1e-08)
    return (new_rows, new_first, new_second)


def per_device(reps, shards, queries, target_ids, negative_ids, table_rows, first_moment, second_moment):
    tokens, width = queries.shape
    uniq = table_rows.shape[0]
    per_target = target_ids.shape[1]
    per_peer = per_target + negative_ids.shape[1]
    bands = shards // BAND
    band_rows = BAND * per_peer
    cands = shards * per_peer
    span = width // CHUNKS
    ids = jnp.concatenate([target_ids, negative_ids], axis=1)
    ids = jnp.tile(ids, (1, 128 // per_peer))[:, None, :]
    dma = pltpu.SemaphoreType.DMA
    vmem = pl.BlockSpec(memory_space=pltpu.VMEM)
    grad_queries, grad = pl.pallas_call(
        functools.partial(kernel, reps, shards, per_target),
        out_shape=(
            jax.ShapeDtypeStruct((tokens, width), F32),
            jax.ShapeDtypeStruct((uniq, width), F32),
        ),
        in_specs=[vmem] * 3,
        out_specs=(vmem, vmem),
        scratch_shapes=[
            pltpu.VMEM((shards, 1, 128), jnp.int32),
            pltpu.VMEM((uniq, width), BF16),
            pltpu.VMEM((bands, uniq, band_rows), BF16),
            pltpu.VMEM((shards, per_peer, width), BF16),
            pltpu.VMEM((shards, per_peer, width), BF16),
            pltpu.VMEM((tokens, width), F32),
            pltpu.VMEM((tokens, 1), F32),
            pltpu.VMEM((tokens, width), BF16),
            pltpu.VMEM((bands, band_rows, width), F32),
            pltpu.VMEM((bands, band_rows, 1), F32),
            pltpu.VMEM((bands, band_rows, width), BF16),
            pltpu.VMEM((bands, band_rows, tokens), F32),
            pltpu.VMEM((bands, band_rows, tokens), BF16),
            pltpu.VMEM((CHUNKS, shards, per_peer, span), BF16),
            pltpu.VMEM((CHUNKS, shards, per_peer, span), BF16),
            pltpu.VMEM((CHUNKS, reps, uniq // reps, span), F32),
            pltpu.VMEM((CHUNKS, reps, uniq // reps, span), F32),
            pltpu.VMEM((CHUNKS, reps, uniq // reps, span), F32),
            dma,
            dma,
            dma,
            dma((bands,)),
            dma,
            dma((CHUNKS,)),
            dma,
            dma((CHUNKS,)),
            dma,
            dma((CHUNKS,)),
            dma,
        ],
        compiler_params=pltpu.CompilerParams(
            collective_id=0, has_side_effects=True, vmem_limit_bytes=56 * 1024 * 1024
        ),
        cost_estimate=pl.CostEstimate(
            flops=2 * width * (3 * tokens * cands + 2 * uniq * cands),
            bytes_accessed=width * (6 * tokens + 8 * uniq),
            transcendentals=tokens * cands,
        ),
    )(ids, queries, table_rows)
    new_rows, new_first, new_second = adam_rows(table_rows, first_moment, second_moment, grad)
    return (new_rows, new_first, new_second, grad_queries)


def solution(mesh):
    return jax.shard_map(
        functools.partial(per_device, mesh.shape["rep"], mesh.shape["shard"]),
        mesh=mesh,
        in_specs=(
            P(("rep", "shard"), None),
            P(("rep", "shard"), None),
            P(("rep", "shard"), None),
            P("shard", None),
            P("shard", None),
            P("shard"),
        ),
        out_specs=(P("shard", None), P("shard", None), P("shard"), P(("rep", "shard"), None)),
        check_vma=False,
    )
```

time: 380 us -> 185 us (0.49)
  the two profiles are of different devices: /device:TPU:6 before, /device:TPU:198 now
where the time goes in v1:
time: 185 us
  Pallas kernels  178 us (96%)
  other arithmetic  4.39 us (2%)
  local copies, waits for them, and re-layouts  1.99 us (1%)
    pallas_call x1, Pallas kernels, per_device(): pl.pallas_call(functools.partial(kernel, reps, shards, per_target), out_s...  178 us

profile of v1, /device:TPU:198, one launch (start us, length us, event | category | flops | bytes accessed | tf_op | source)
XLA Modules:
  0.0 185.0 jit_solution(16122783734229088222)
XLA Ops:
  0.6 0.7 pad_add_fusion
  1.4 0.7 copy.11.ids_ref
  2.0 0.0 copy-start.4
  2.0 0.0 copy-start.2
  2.1 0.0 copy-start.3
  2.1 177.9 %shard_map.93 = (f32[768,512]{1,0:T(8,128)}, f32[512,512]{1,0:T(8,128)}) custom-call(s32[48,1,128]{2,1,0:T(1,128)} %copy.11.ids_ref, bf16[768,512]{1,0:T(8,128)(2,1)} %q_ref.1, f32[512,512]{1,0:T(8,128)} %table_ref.1), custom_call_target="tpu_custom_call" | custom-call | flops 5234491392 | bytes 4456448 | tf_op jit(solution)/shard_map/pallas_call | solution.py:349
  180.0 0.0 copy-start
  180.0 1.5 multiply_reduce_fusion
  181.5 0.0 copy-done.4
  181.5 0.6 sqrt_add_fusion
  182.1 0.0 copy-done.2
  182.1 0.0 copy-done.3
  182.1 0.0 copy-done
  182.1 0.0 copy-start.1
  182.1 1.6 divide_subtract_fusion
  183.7 0.1 copy-done.1
  183.8 1.1 copy.13
  (1 shorter events, 0.0 us)
Async XLA Ops:
  2.0 179.4 %copy-start.4 = (f32[512]{0:T(512)S(1)}, f32[512]{0:T(512)}, u32[]{:S(2)}) copy-start(f32[512]{0:T(512)} %param.11) | copy-start | bytes 6148
  2.0 180.0 %copy-start.2 = (f32[512,512]{1,0:T(8,128)S(1)}, f32[512,512]{1,0:T(8,128)}, u32[]{:S(2)}) copy-start(f32[512,512]{1,0:T(8,128)} %table_ref.1) | copy-start | bytes 3145732
  2.1 180.0 %copy-start.3 = (f32[512,512]{1,0:T(8,128)S(1)}, f32[512,512]{1,0:T(8,128)}, u32[]{:S(2)}) copy-start(f32[512,512]{1,0:T(8,128)} %param.10) | copy-start | bytes 3145732
  180.0 2.1 %copy-start = (f32[512,512]{1,0:T(8,128)S(1)}, f32[512,512]{1,0:T(8,128)}, u32[]{:S(2)}) copy-start(f32[512,512]{1,0:T(8,128)} %get-tuple-element.6) | copy-start | bytes 3145732
  182.1 1.8 copy-start.1

commit v2 on v1

v2 whole, which is shorter than its diff:
```python
import functools

import jax
import jax.numpy as jnp
from jax import lax
from jax.experimental import pallas as pl
from jax.experimental.pallas import tpu as pltpu
from jax.sharding import PartitionSpec as P

SCALE = 72.0
EPS = 1e-06
CHUNKS = 4
PIECES = 2
LOW = 2
CORES = 2
QUAD = 4
GROUP = 4
BAND = 8
F32 = jnp.float32
BF16 = jnp.bfloat16
NT = (((1,), (1,)), ((), ()))
TN = (((0,), (0,)), ((), ()))


def iota(shape, axis):
    return lax.broadcasted_iota(jnp.int32, shape, axis)


def push(src, dst, send, recv, device):
    return pltpu.make_async_remote_copy(
        src_ref=src,
        dst_ref=dst,
        send_sem=send,
        recv_sem=recv,
        device_id=device,
        device_id_type=pl.DeviceIdType.MESH,
    )


def kernel(
    reps,
    shards,
    per_target,
    ids_ref,
    q_ref,
    table_ref,
    gq_ref,
    grad_ref,
    ids_in,
    ids_plane,
    minus,
    plus,
    stage,
    onehot_t,
    arrived,
    query_unit,
    query_norm,
    query_bf,
    cand_unit,
    cand_norm,
    cand_bf,
    weights,
    coef,
    back,
    came,
    local,
    parts,
    gathered,
    ids_send,
    ids_recv,
    plane_send,
    plane_recv,
    ring_send,
    minus_recv,
    plus_recv,
    rows_send,
    rows_recv,
    back_send,
    back_recv,
    part_send,
    part_recv,
    full_send,
    full_recv,
):
    me = lax.axis_index("shard")
    rep = lax.axis_index("rep")
    per_peer = came.shape[2]
    uniq, width = table_ref.shape
    tokens = query_bf.shape[0]
    depth = shards // QUAD
    bands = depth // 2
    band_rows = BAND * per_peer
    lanes = 128
    per_pack = lanes // per_peer
    span = width // CHUNKS
    slice_rows = uniq // reps
    columns = width // GROUP
    members = GROUP * QUAD
    piece = uniq // PIECES

    z = me // CORES % depth
    my_quad = me // (CORES * depth) * CORES + me % CORES
    long = reps // LOW
    pair = rep % long // 2 * 2
    my_slice = rep // long * 2 + rep % 2
    my_place = my_slice * QUAD + my_quad

    def shard_at(quad, level):
        return quad // CORES * (CORES * depth) + level * CORES + quad % CORES

    def member(place):
        part = place // QUAD
        return {"rep": part // 2 * long + pair + part % 2, "shard": shard_at(place % QUAD, z)}

    def to_shards(body):
        def step(k, carry):
            body(lax.rem(me + k, shards))
            return carry

        lax.fori_loop(1, shards, step, 0)

    def to_reps(body):
        def step(k, carry):
            body(lax.rem(rep + k, reps))
            return carry

        lax.fori_loop(1, reps, step, 0)

    def to_members(body):
        def step(k, carry):
            body(lax.rem(my_place + k, members))
            return carry

        lax.fori_loop(1, members, step, 0)

    barrier = pltpu.get_barrier_semaphore()

    def hello(device):
        pl.semaphore_signal(
            barrier, inc=1, device_id=device, device_id_type=pl.DeviceIdType.MESH
        )

    def hello_member(place):
        @pl.when((place // QUAD != my_slice) & (place % QUAD != my_quad))
        def _():
            hello(member(place))

    to_shards(lambda p: hello({"shard": p}))
    to_reps(lambda p: hello({"rep": p}))
    to_members(hello_member)
    mine = pl.ds(pl.multiple_of(my_slice * columns, columns), columns)
    plus[0] = table_ref[:, mine].astype(BF16)
    pl.semaphore_wait(barrier, shards + reps - 2 + (GROUP - 1) * (QUAD - 1))

    up = {"shard": shard_at(my_quad, lax.rem(z + 1, depth))}
    down = {"shard": shard_at(my_quad, lax.rem(z + depth - 1, depth))}

    def rows_of(h):
        return pl.ds(h * piece, piece)

    def climb(src, step, h):
        return push(src, minus.at[step, rows_of(h)], ring_send, minus_recv.at[step, h], up)

    def sink(src, step, h):
        return push(src, plus.at[step, rows_of(h)], ring_send, plus_recv.at[step, h], down)

    for h in range(PIECES):
        climb(plus.at[0, rows_of(h)], 0, h).start()
        sink(plus.at[0, rows_of(h)], 1, h).start()
    to_members(
        lambda p: push(
            ids_ref.at[lax.rem(p, QUAD)],
            ids_plane.at[my_place],
            plane_send,
            plane_recv,
            member(p),
        ).start()
    )
    ids_plane[my_place] = ids_ref[my_quad]
    to_shards(
        lambda p: push(
            ids_ref.at[p // (CORES * depth) * CORES + p % CORES, p // CORES % depth],
            ids_in.at[me],
            ids_send,
            ids_recv,
            {"shard": p},
        ).start()
    )
    ids_in[me] = ids_ref[my_quad, z]

    values = q_ref[...].astype(F32)
    norm = jnp.sqrt(jnp.sum(values * values, axis=-1, keepdims=True) + EPS)
    unit = values / norm
    query_norm[...] = norm
    query_unit[...] = unit
    query_bf[...] = unit.astype(BF16)

    others = pl.ds(0, members - 1)
    push(ids_plane.at[others], ids_plane.at[others], plane_send, plane_recv, up).wait()

    def serve(band, half, table, level):
        which = iota((1, lanes), 1) // per_peer
        tall = []
        for pack in range(members // per_pack):
            row = ids_plane[pack * per_pack, level]
            for j in range(1, per_pack):
                row = jnp.where(which == j, ids_plane[pack * per_pack + j, level], row)
            tall.append(jnp.transpose(jnp.broadcast_to(row, (lanes, lanes))))
        column = jnp.concatenate(tall, axis=0)
        column = jnp.concatenate([column] * (uniq // lanes), axis=1)
        onehot = jnp.where(iota((members * per_peer, uniq), 1) == column, 1.0, 0.0).astype(BF16)
        rows = jnp.dot(onehot, table[...], preferred_element_type=F32).astype(BF16)
        stage[band, :, half] = rows.reshape(members, per_peer, columns)

    def gather(band, carry):
        for h in range(PIECES):
            step = climb(minus.at[band, rows_of(h)], band, h)
            step.wait_recv()

            @pl.when(band < bands - 1)
            def _():
                climb(minus.at[band, rows_of(h)], band + 1, h).start()

        for h in range(PIECES):

            @pl.when(band < bands - 1)
            def _():
                sink(plus.at[band + 1, rows_of(h)], band + 1, h).wait_recv()

            @pl.when(band < bands - 2)
            def _():
                sink(plus.at[band + 1, rows_of(h)], band + 2, h).start()

        serve(band, 0, minus.at[band], lax.rem(z + depth - band - 1, depth))
        serve(band, 1, plus.at[band], lax.rem(z + band, depth))
        there = arrived.at[band, my_slice, my_quad]
        to_members(
            lambda p: push(
                stage.at[band, p], there, rows_send, rows_recv.at[band], member(p)
            ).start()
        )
        pltpu.make_async_copy(stage.at[band, my_place], there, rows_recv.at[band]).start()
        return carry

    lax.fori_loop(0, bands, gather, 0)

    def score(band, total):
        push(arrived.at[band], arrived.at[band], rows_send, rows_recv.at[band], up).wait_recv()
        values = jnp.concatenate(
            [arrived[band, part].reshape(band_rows, columns) for part in range(GROUP)], axis=1
        ).astype(F32)
        norm = jnp.sqrt(jnp.sum(values * values, axis=-1, keepdims=True) + EPS)
        unit = values / norm
        unit_bf = unit.astype(BF16)
        cand_norm[band] = norm
        cand_unit[band] = unit
        cand_bf[band] = unit_bf
        scores = lax.dot_general(unit_bf, query_bf[...], NT, preferred_element_type=F32) * SCALE
        weight = jnp.exp(scores)
        weights[band] = weight
        return total + jnp.sum(weight, axis=0, keepdims=True)

    total = lax.fori_loop(0, bands, score, jnp.zeros((1, tokens), F32))
    share = 1.0 / total

    def owner_of(band, entry):
        level = z + depth - band - 1 if entry % 2 == 0 else z + band
        return shard_at(entry // 2, lax.rem(level, depth))

    def send_back(chunk, band, entry):
        peer = owner_of(band, entry)

        @pl.when(peer != me)
        def _():
            push(
                back.at[chunk, band, entry],
                came.at[chunk, me],
                back_send,
                back_recv.at[chunk],
                {"shard": peer},
            ).start()

    def row_grads(band, carry):
        place = iota((band_rows, 1), 0)
        quad = place // (2 * per_peer)
        level = jnp.where(place // per_peer % 2 == 1, z + band, z + depth - band - 1)
        level = jnp.where(level >= depth, level - depth, level)
        slot = place % per_peer
        target = jnp.where(slot < per_target, shard_at(quad, level) * per_target + slot, -1)
        label = jnp.where(iota((band_rows, tokens), 1) == target, 1.0, 0.0)
        coef_band = (weights[band] * share - label).astype(BF16)
        coef[band] = coef_band
        grad = jnp.dot(coef_band, query_bf[...], preferred_element_type=F32) * SCALE
        unit = cand_unit[band]
        grad = (grad - unit * jnp.sum(unit * grad, axis=-1, keepdims=True)) / cand_norm[band]
        grad = grad.astype(BF16)
        for chunk in range(CHUNKS):
            back[chunk, band] = grad[:, chunk * span : (chunk + 1) * span].reshape(
                BAND, per_peer, span
            )
        for entry in range(BAND):
            send_back(0, band, entry)
        return carry

    lax.fori_loop(0, bands, row_grads, 0)
    for chunk in range(1, CHUNKS):

        def later(band, carry):
            for entry in range(BAND):
                send_back(chunk, band, entry)
            return carry

        lax.fori_loop(0, bands, later, 0)
    for chunk in range(CHUNKS):
        pltpu.make_async_copy(
            back.at[chunk, 0, 2 * my_quad + 1], came.at[chunk, me], back_recv.at[chunk]
        ).start()

    others = pl.ds(0, shards - 1)
    push(ids_in.at[others], ids_in.at[others], ids_send, ids_recv, up).wait()

    def mark(block, carry):
        which = iota((1, lanes), 1) // per_peer
        flat = []
        for pack in range(band_rows // lanes):
            first = block * BAND + pack * per_pack
            row = ids_in[first]
            for j in range(1, per_pack):
                row = jnp.where(which == j, ids_in[first + j], row)
            flat.append(row)
        row = jnp.concatenate(flat, axis=1)
        onehot_t[block] = jnp.where(iota((uniq, band_rows), 0) == row, 1.0, 0.0).astype(BF16)
        return carry

    lax.fori_loop(0, bands, mark, 0)

    tile = 256 if tokens % 256 == 0 else 128

    def query_grads(i, carry):
        at = pl.ds(pl.multiple_of(i * tile, tile), tile)
        grad = jnp.zeros((tile, width), F32)
        for band in range(bands):
            grad += lax.dot_general(
                coef[band, :, at], cand_bf[band], TN, preferred_element_type=F32
            )
        grad = grad * SCALE
        unit = query_unit[at]
        gq_ref[at] = (grad - unit * jnp.sum(unit * grad, axis=-1, keepdims=True)) / query_norm[at]
        return carry

    lax.fori_loop(0, tokens // tile, query_grads, 0)

    def reduce_chunk(chunk):
        push(
            came.at[chunk], came.at[chunk], back_send, back_recv.at[chunk], up
        ).wait_recv()
        for half in range(2):
            rows = pl.ds(half * (uniq // 2), uniq // 2)
            grad = jnp.zeros((uniq // 2, span), F32)
            for band in range(bands):
                grad += jnp.dot(
                    onehot_t[band, rows, :],
                    came[chunk, pl.ds(band * BAND, BAND)].reshape(band_rows, span),
                    preferred_element_type=F32,
                )
            local[chunk, pl.ds(half * (reps // 2), reps // 2)] = grad.reshape(
                reps // 2, slice_rows, span
            )
        to_reps(
            lambda p: push(
                local.at[chunk, p], parts.at[chunk, rep], part_send, part_recv.at[chunk], {"rep": p}
            ).start()
        )

    def share_chunk(chunk):
        other = pl.ds(0, reps - 1)
        push(
            parts.at[chunk, other],
            parts.at[chunk, other],
            part_send,
            part_recv.at[chunk],
            up,
        ).wait_recv()
        parts[chunk, rep] = local[chunk, rep]
        gathered[chunk, rep] = jnp.sum(parts[chunk], axis=0)
        to_reps(
            lambda p: push(
                gathered.at[chunk, rep],
                gathered.at[chunk, rep],
                full_send,
                full_recv.at[chunk],
                {"rep": p},
            ).start()
        )

    def finish_chunk(chunk):
        other = pl.ds(0, reps - 1)
        push(
            gathered.at[chunk, other],
            gathered.at[chunk, other],
            full_send,
            full_recv.at[chunk],
            up,
        ).wait_recv()
        grad_ref[:, chunk * span : (chunk + 1) * span] = gathered[chunk].reshape(uniq, span)

    for chunk in range(CHUNKS):
        reduce_chunk(chunk)
        share_chunk(chunk)
    for chunk in range(CHUNKS):
        finish_chunk(chunk)

    push(plus.at[pl.ds(0, bands - 1)], plus.at[pl.ds(0, bands - 1)], ring_send, ids_recv, up).wait_send()
    push(minus, minus, ring_send, ids_recv, up).wait_send()
    other = pl.ds(0, members - 1)
    for band in range(bands):
        push(stage.at[band, other], stage.at[band, other], rows_send, ids_recv, up).wait_send()
    for chunk in range(CHUNKS):
        other = pl.ds(0, shards - 1)
        push(came.at[chunk, other], came.at[chunk, other], back_send, ids_recv, up).wait_send()
        other = pl.ds(0, reps - 1)
        push(local.at[chunk, other], local.at[chunk, other], part_send, ids_recv, up).wait_send()
        push(
            gathered.at[chunk, other], gathered.at[chunk, other], full_send, ids_recv, up
        ).wait_send()


def adam_rows(rows, first, second, grad):
    new_first = 0.9 * first + 0.1 * grad
    new_second = 0.999 * second + 0.001 * jnp.mean(grad * grad, axis=-1)
    new_rows = rows - 0.01 * new_first / (jnp.sqrt(new_second)[:, None] + 1e-08)
    return (new_rows, new_first, new_second)


def per_device(reps, shards, queries, target_ids, negative_ids, table_rows, first_moment, second_moment):
    tokens, width = queries.shape
    uniq = table_rows.shape[0]
    per_target = target_ids.shape[1]
    per_peer = per_target + negative_ids.shape[1]
    bands = shards // BAND
    band_rows = BAND * per_peer
    cands = shards * per_peer
    span = width // CHUNKS
    ids = jnp.concatenate([target_ids, negative_ids], axis=1)
    depth = shards // QUAD
    ids = jnp.tile(ids, (1, 128 // per_peer)).reshape(QUAD // CORES, depth, CORES, 128)
    ids = ids.transpose(0, 2, 1, 3).reshape(QUAD, depth, 1, 128)
    members = GROUP * QUAD
    columns = width // GROUP
    dma = pltpu.SemaphoreType.DMA
    vmem = pl.BlockSpec(memory_space=pltpu.VMEM)
    grad_queries, grad = pl.pallas_call(
        functools.partial(kernel, reps, shards, per_target),
        out_shape=(
            jax.ShapeDtypeStruct((tokens, width), F32),
            jax.ShapeDtypeStruct((uniq, width), F32),
        ),
        in_specs=[vmem] * 3,
        out_specs=(vmem, vmem),
        scratch_shapes=[
            pltpu.VMEM((shards, 1, 128), jnp.int32),
            pltpu.VMEM((members, depth, 1, 128), jnp.int32),
            pltpu.VMEM((bands, uniq, columns), BF16),
            pltpu.VMEM((bands, uniq, columns), BF16),
            pltpu.VMEM((bands, members, 2, per_peer, columns), BF16),
            pltpu.VMEM((bands, uniq, band_rows), BF16),
            pltpu.VMEM((bands, GROUP, QUAD, 2, per_peer, columns), BF16),
            pltpu.VMEM((tokens, width), F32),
            pltpu.VMEM((tokens, 1), F32),
            pltpu.VMEM((tokens, width), BF16),
            pltpu.VMEM((bands, band_rows, width), F32),
            pltpu.VMEM((bands, band_rows, 1), F32),
            pltpu.VMEM((bands, band_rows, width), BF16),
            pltpu.VMEM((bands, band_rows, tokens), F32),
            pltpu.VMEM((bands, band_rows, tokens), BF16),
            pltpu.VMEM((CHUNKS, bands, BAND, per_peer, span), BF16),
            pltpu.VMEM((CHUNKS, shards, per_peer, span), BF16),
            pltpu.VMEM((CHUNKS, reps, uniq // reps, span), F32),
            pltpu.VMEM((CHUNKS, reps, uniq // reps, span), F32),
            pltpu.VMEM((CHUNKS, reps, uniq // reps, span), F32),
            dma,
            dma,
            dma,
            dma,
            dma,
            dma((bands, PIECES)),
            dma((bands, PIECES)),
            dma,
            dma((bands,)),
            dma,
            dma((CHUNKS,)),
            dma,
            dma((CHUNKS,)),
            dma,
            dma((CHUNKS,)),
        ],
        compiler_params=pltpu.CompilerParams(
            collective_id=0, has_side_effects=True, vmem_limit_bytes=56 * 1024 * 1024
        ),
        cost_estimate=pl.CostEstimate(
            flops=2 * width * (3 * tokens * cands + 2 * uniq * cands),
            bytes_accessed=width * (6 * tokens + 8 * uniq),
            transcendentals=tokens * cands,
        ),
    )(ids, queries, table_rows)
    new_rows, new_first, new_second = adam_rows(table_rows, first_moment, second_moment, grad)
    return (new_rows, new_first, new_second, grad_queries)


def solution(mesh):
    return jax.shard_map(
        functools.partial(per_device, mesh.shape["rep"], mesh.shape["shard"]),
        mesh=mesh,
        in_specs=(
            P(("rep", "shard"), None),
            P(("rep", "shard"), None),
            P(("rep", "shard"), None),
            P("shard", None),
            P("shard", None),
            P("shard"),
        ),
        out_specs=(P("shard", None), P("shard", None), P("shard"), P(("rep", "shard"), None)),
        check_vma=False,
    )
```

time: 185 us -> 144 us (0.78)
  the two profiles are of different devices: /device:TPU:198 before, /device:TPU:6 now
where the time goes in v2:
time: 144 us; the launch traced here: 142 us
  Pallas kernels  135 us (94%)
  other arithmetic  4.39 us (3%)
  local copies, waits for them, and re-layouts  2.16 us (2%)
    pallas_call x1, Pallas kernels, per_device(): pl.pallas_call(functools.partial(kernel, reps, shards, per_target), out_s...  135 us

profile of v2, /device:TPU:6, one launch (start us, length us, event | category | flops | bytes accessed | tf_op | source)
XLA Modules:
  0.0 141.8 jit_solution(7697601276749978158)
XLA Ops:
  0.6 0.7 pad_add_fusion
  1.4 0.1 copy.11
  1.5 0.1 tile.9
  1.6 0.6 copy.13.ids_ref
  2.2 0.0 copy-start.4
  2.2 0.0 copy-start.2
  2.2 0.0 copy-start.3
  2.2 134.5 %shard_map.93 = (f32[768,512]{1,0:T(8,128)}, f32[512,512]{1,0:T(8,128)}) custom-call(s32[4,12,1,128]{3,2,1,0:T(1,128)} %copy.13.ids_ref, bf16[768,512]{1,0:T(8,128)(2,1)} %q_ref.1, f32[512,512]{1,0:T(8,128)} %table_ref.1), custom_call_target="tpu_custom_call" | custom-call | flops 5234491392 | bytes 4456448 | tf_op jit(solution)/shard_map/pallas_call | solution.py:452
  136.8 0.0 copy-start
  136.8 1.5 %multiply_reduce_fusion = f32[512]{0:T(512)S(1)} fusion(f32[512,512]{1,0:T(8,128)} %get-tuple-element.6), kind=kLoop, calls=%fused_computation.1 | loop fusion | flops 523776 | bytes 1050624 | tf_op jit(solution)/shard_map/reduce_sum | solution.py:430
  138.3 0.0 copy-done.4
  138.3 0.6 sqrt_add_fusion
  138.8 0.0 copy-done.2
  138.8 0.0 copy-done.3
  138.8 0.0 copy-done
  138.9 0.0 copy-start.1
  138.9 1.6 %divide_subtract_fusion = (f32[512,512]{1,0:T(8,128)}, f32[512,512]{1,0:T(8,128)}) fusion(f32[512,512]{1,0:T(8,128)S(1)} %copy-done.2, f32[512]{0:T(512)S(1)} %get-tuple-element.10, f32[512,512]{1,0:T(8,128)S(1)} %copy-done, f32[512,512]{1,0:T(8,128)S(1)} %copy-done.3), kind=kLoop, calls=%fused_computation | loop fusion | flops 1572864 | bytes 5244928 | tf_op jit(solution)/shard_map/sub | solution.py:431
  140.5 0.1 copy-done.1
  140.6 1.1 copy.15
  (2 shorter events, 0.0 us)
Async XLA Ops:
  2.2 136.0 %copy-start.4 = (f32[512]{0:T(512)S(1)}, f32[512]{0:T(512)}, u32[]{:S(2)}) copy-start(f32[512]{0:T(512)} %param.11) | copy-start | bytes 6148
  2.2 136.6 %copy-start.2 = (f32[512,512]{1,0:T(8,128)S(1)}, f32[512,512]{1,0:T(8,128)}, u32[]{:S(2)}) copy-start(f32[512,512]{1,0:T(8,128)} %table_ref.1) | copy-start | bytes 3145732
  2.2 136.6 %copy-start.3 = (f32[512,512]{1,0:T(8,128)S(1)}, f32[512,512]{1,0:T(8,128)}, u32[]{:S(2)}) copy-start(f32[512,512]{1,0:T(8,128)} %param.10) | copy-start | bytes 3145732
  136.8 2.1 %copy-start = (f32[512,512]{1,0:T(8,128)S(1)}, f32[512,512]{1,0:T(8,128)}, u32[]{:S(2)}) copy-start(f32[512,512]{1,0:T(8,128)} %get-tuple-element.6) | copy-start | bytes 3145732
  138.9 1.8 %copy-start.1 = (f32[768,512]{1,0:T(8,128)S(1)}, f32[768,512]{1,0:T(8,128)}, u32[]{:S(2)}) copy-start(f32[768,512]{1,0:T(8,128)} %get-tuple-element.19) | copy-start | bytes 4718596

commit v3 on v2

--- a/solution.py
+++ b/solution.py
@@ -11,6 +11,7 @@
 EPS = 1e-06
 CHUNKS = 4
 PIECES = 2
+STAGED = 3
 LOW = 2
 CORES = 2
 QUAD = 4
@@ -41,11 +42,16 @@
     reps,
     shards,
     per_target,
-    ids_ref,
+    targets_ref,
+    negatives_ref,
     q_ref,
     table_ref,
+    gq_out,
+    grad_out,
+    square_ref,
+    ids_ref,
     gq_ref,
-    grad_ref,
+    out_sem,
     ids_in,
     ids_plane,
     minus,
@@ -81,6 +87,10 @@
     part_recv,
     full_send,
     full_recv,
+    crossed,
+    cross_send,
+    cross_recv,
+    half_recv,
 ):
     me = lax.axis_index("shard")
     rep = lax.axis_index("rep")
@@ -148,8 +158,20 @@
     to_shards(lambda p: hello({"shard": p}))
     to_reps(lambda p: hello({"rep": p}))
     to_members(hello_member)
+    asked = jnp.concatenate([targets_ref[...], negatives_ref[...]] * per_pack, axis=0)
+    blank = jnp.zeros((lanes, lanes - shards), jnp.int32)
+    asked = jnp.transpose(jnp.concatenate([asked, blank], axis=1))
+    for owner in range(shards):
+        quad = owner // (CORES * depth) * CORES + owner % CORES
+        ids_ref[quad, owner // CORES % depth] = asked[owner : owner + 1]
     mine = pl.ds(pl.multiple_of(my_slice * columns, columns), columns)
     plus[0] = table_ref[:, mine].astype(BF16)
+    values = q_ref[...].astype(F32)
+    norm = jnp.sqrt(jnp.sum(values * values, axis=-1, keepdims=True) + EPS)
+    unit = values / norm
+    query_norm[...] = norm
+    query_unit[...] = unit
+    query_bf[...] = unit.astype(BF16)
     pl.semaphore_wait(barrier, shards + reps - 2 + (GROUP - 1) * (QUAD - 1))
 
     up = {"shard": shard_at(my_quad, lax.rem(z + 1, depth))}
@@ -177,27 +199,6 @@
         ).start()
     )
     ids_plane[my_place] = ids_ref[my_quad]
-    to_shards(
-        lambda p: push(
-            ids_ref.at[p // (CORES * depth) * CORES + p % CORES, p // CORES % depth],
-            ids_in.at[me],
-            ids_send,
-            ids_recv,
-            {"shard": p},
-        ).start()
-    )
-    ids_in[me] = ids_ref[my_quad, z]
-
-    values = q_ref[...].astype(F32)
-    norm = jnp.sqrt(jnp.sum(values * values, axis=-1, keepdims=True) + EPS)
-    unit = values / norm
-    query_norm[...] = norm
-    query_unit[...] = unit
-    query_bf[...] = unit.astype(BF16)
-
-    others = pl.ds(0, members - 1)
-    push(ids_plane.at[others], ids_plane.at[others], plane_send, plane_recv, up).wait()
-
     def serve(band, half, table, level):
         which = iota((1, lanes), 1) // per_peer
         tall = []
@@ -212,26 +213,29 @@
         rows = jnp.dot(onehot, table[...], preferred_element_type=F32).astype(BF16)
         stage[band, :, half] = rows.reshape(members, per_peer, columns)
 
+    def hop(band, h):
+        @pl.when(band < bands)
+        def _():
+            climb(minus.at[band, rows_of(h)], band, h).wait_recv()
+
+        @pl.when(band < bands - 1)
+        def _():
+            climb(minus.at[band, rows_of(h)], band + 1, h).start()
+            sink(plus.at[band + 1, rows_of(h)], band + 1, h).wait_recv()
+
+        @pl.when(band < bands - 2)
+        def _():
+            sink(plus.at[band + 1, rows_of(h)], band + 2, h).start()
+
+    for h in range(PIECES):
+        hop(0, h)
+    others = pl.ds(0, members - 1)
+    push(ids_plane.at[others], ids_plane.at[others], plane_send, plane_recv, up).wait()
+
     def gather(band, carry):
-        for h in range(PIECES):
-            step = climb(minus.at[band, rows_of(h)], band, h)
-            step.wait_recv()
-
-            @pl.when(band < bands - 1)
-            def _():
-                climb(minus.at[band, rows_of(h)], band + 1, h).start()
-
-        for h in range(PIECES):
-
-            @pl.when(band < bands - 1)
-            def _():
-                sink(plus.at[band + 1, rows_of(h)], band + 1, h).wait_recv()
-
-            @pl.when(band < bands - 2)
-            def _():
-                sink(plus.at[band + 1, rows_of(h)], band + 2, h).start()
-
         serve(band, 0, minus.at[band], lax.rem(z + depth - band - 1, depth))
+        for h in range(PIECES // 2):
+            hop(band + 1, h)
         serve(band, 1, plus.at[band], lax.rem(z + band, depth))
         there = arrived.at[band, my_slice, my_quad]
         to_members(
@@ -240,9 +244,21 @@
             ).start()
         )
         pltpu.make_async_copy(stage.at[band, my_place], there, rows_recv.at[band]).start()
+        for h in range(PIECES // 2, PIECES):
+            hop(band + 1, h)
         return carry
 
     lax.fori_loop(0, bands, gather, 0)
+    to_shards(
+        lambda p: push(
+            ids_ref.at[p // (CORES * depth) * CORES + p % CORES, p // CORES % depth],
+            ids_in.at[me],
+            ids_send,
+            ids_recv,
+            {"shard": p},
+        ).start()
+    )
+    ids_in[me] = ids_ref[my_quad, z]
 
     def score(band, total):
         push(arrived.at[band], arrived.at[band], rows_send, rows_recv.at[band], up).wait_recv()
@@ -349,6 +365,7 @@
         return carry
 
     lax.fori_loop(0, tokens // tile, query_grads, 0)
+    pltpu.make_async_copy(gq_ref, gq_out, out_sem.at[CHUNKS]).start()
 
     def reduce_chunk(chunk):
         push(
@@ -366,49 +383,126 @@
             local[chunk, pl.ds(half * (reps // 2), reps // 2)] = grad.reshape(
                 reps // 2, slice_rows, span
             )
-        to_reps(
+        if chunk < STAGED:
+            push(
+                local.at[chunk, their_half], crossed.at[chunk], cross_send, cross_recv.at[chunk], across
+            ).start()
+        else:
+            to_reps(
+                lambda p: push(
+                    local.at[chunk, p], parts.at[chunk, rep], part_send, part_recv.at[chunk], {"rep": p}
+                ).start()
+            )
+
+    across = {"rep": lax.rem(rep + long, reps)}
+    low = rep // long
+    row = rep % long
+    my_half = pl.ds(low * long, long)
+    my_rows = pl.ds(pl.multiple_of(rep * slice_rows, 8), slice_rows)
+    half_rows = pl.ds(pl.multiple_of(low * long * slice_rows, 8), long * slice_rows)
+    their_half = pl.ds((1 - low) * long, long)
+
+    def to_long(body):
+        def step(k, carry):
+            body(lax.rem(row + k, long))
+            return carry
+
+        lax.fori_loop(1, long, step, 0)
+
+    def fold_chunk(chunk):
+        push(
+            crossed.at[chunk], crossed.at[chunk], cross_send, cross_recv.at[chunk], across
+        ).wait_recv()
+        local[chunk, my_half] += crossed[chunk]
+        to_long(
             lambda p: push(
-                local.at[chunk, p], parts.at[chunk, rep], part_send, part_recv.at[chunk], {"rep": p}
+                local.at[chunk, low * long + p],
+                parts.at[chunk, row],
+                part_send,
+                part_recv.at[chunk],
+                {"rep": low * long + p},
             ).start()
         )
 
     def share_chunk(chunk):
-        other = pl.ds(0, reps - 1)
+        count = long if chunk < STAGED else reps
+        here = row if chunk < STAGED else rep
+        other = pl.ds(0, count - 1)
         push(
-            parts.at[chunk, other],
-            parts.at[chunk, other],
-            part_send,
-            part_recv.at[chunk],
-            up,
+            parts.at[chunk, other], parts.at[chunk, other], part_send, part_recv.at[chunk], up
         ).wait_recv()
-        parts[chunk, rep] = local[chunk, rep]
-        gathered[chunk, rep] = jnp.sum(parts[chunk], axis=0)
-        to_reps(
-            lambda p: push(
-                gathered.at[chunk, rep],
-                gathered.at[chunk, rep],
+        parts[chunk, here] = local[chunk, rep]
+        gathered[chunk, my_rows] = jnp.sum(parts[chunk, pl.ds(0, count)], axis=0)
+
+        def give(p):
+            push(
+                gathered.at[chunk, my_rows],
+                gathered.at[chunk, my_rows],
                 full_send,
                 full_recv.at[chunk],
                 {"rep": p},
             ).start()
+
+        if chunk < STAGED:
+            to_long(lambda p: give(low * long + p))
+        else:
+            to_reps(give)
+
+    def pass_chunk(chunk):
+        other = pl.ds(0, (long - 1) * slice_rows)
+        push(
+            gathered.at[chunk, other], gathered.at[chunk, other], full_send, full_recv.at[chunk], up
+        ).wait_recv()
+        push(
+            gathered.at[chunk, half_rows],
+            gathered.at[chunk, half_rows],
+            cross_send,
+            half_recv.at[chunk],
+            across,
+        ).start()
+
+    def to_grad(chunk):
+        return pltpu.make_async_copy(
+            gathered.at[chunk],
+            grad_out.at[:, pl.ds(chunk * span, span)],
+            out_sem.at[chunk],
         )
 
     def finish_chunk(chunk):
-        other = pl.ds(0, reps - 1)
-        push(
-            gathered.at[chunk, other],
-            gathered.at[chunk, other],
-            full_send,
-            full_recv.at[chunk],
-            up,
-        ).wait_recv()
-        grad_ref[:, chunk * span : (chunk + 1) * span] = gathered[chunk].reshape(uniq, span)
+        if chunk < STAGED:
+            push(
+                gathered.at[chunk, half_rows],
+                gathered.at[chunk, half_rows],
+                cross_send,
+                half_recv.at[chunk],
+                across,
+            ).wait_recv()
+        else:
+            other = pl.ds(0, (reps - 1) * slice_rows)
+            push(
+                gathered.at[chunk, other],
+                gathered.at[chunk, other],
+                full_send,
+                full_recv.at[chunk],
+                up,
+            ).wait_recv()
+        to_grad(chunk).start()
+        part = gathered[chunk]
+        return jnp.sum(part * part, axis=-1, keepdims=True)
 
     for chunk in range(CHUNKS):
         reduce_chunk(chunk)
+        if 0 < chunk <= STAGED:
+            pass_chunk(chunk - 1)
+        if chunk < STAGED:
+            fold_chunk(chunk)
         share_chunk(chunk)
+    if STAGED == CHUNKS:
+        pass_chunk(CHUNKS - 1)
+    square = jnp.zeros((uniq, 1), F32)
     for chunk in range(CHUNKS):
-        finish_chunk(chunk)
+        square += finish_chunk(chunk)
+    square_ref[...] = jnp.broadcast_to(square, (uniq, lanes))
 
     push(plus.at[pl.ds(0, bands - 1)], plus.at[pl.ds(0, bands - 1)], ring_send, ids_recv, up).wait_send()
     push(minus, minus, ring_send, ids_recv, up).wait_send()
@@ -418,16 +512,24 @@
     for chunk in range(CHUNKS):
         other = pl.ds(0, shards - 1)
         push(came.at[chunk, other], came.at[chunk, other], back_send, ids_recv, up).wait_send()
-        other = pl.ds(0, reps - 1)
+        other = pl.ds(0, (long if chunk < STAGED else reps) - 1)
         push(local.at[chunk, other], local.at[chunk, other], part_send, ids_recv, up).wait_send()
+        other = pl.ds(0, ((long if chunk < STAGED else reps) - 1) * slice_rows)
         push(
             gathered.at[chunk, other], gathered.at[chunk, other], full_send, ids_recv, up
         ).wait_send()
-
-
-def adam_rows(rows, first, second, grad):
+        if chunk < STAGED:
+            push(local.at[chunk, their_half], crossed.at[chunk], cross_send, ids_recv, up).wait_send()
+            push(
+                gathered.at[chunk, half_rows], gathered.at[chunk, half_rows], cross_send, ids_recv, up
+            ).wait_send()
+        to_grad(chunk).wait()
+    pltpu.make_async_copy(gq_ref, gq_out, out_sem.at[CHUNKS]).wait()
+
+
+def adam_rows(rows, first, second, grad, square):
     new_first = 0.9 * first + 0.1 * grad
-    new_second = 0.999 * second + 0.001 * jnp.mean(grad * grad, axis=-1)
+    new_second = 0.999 * second + 0.001 * (square[:, 0] / grad.shape[1])
     new_rows = rows - 0.01 * new_first / (jnp.sqrt(new_second)[:, None] + 1e-08)
     return (new_rows, new_first, new_second)
 
@@ -441,23 +543,24 @@
     band_rows = BAND * per_peer
     cands = shards * per_peer
     span = width // CHUNKS
-    ids = jnp.concatenate([target_ids, negative_ids], axis=1)
     depth = shards // QUAD
-    ids = jnp.tile(ids, (1, 128 // per_peer)).reshape(QUAD // CORES, depth, CORES, 128)
-    ids = ids.transpose(0, 2, 1, 3).reshape(QUAD, depth, 1, 128)
     members = GROUP * QUAD
     columns = width // GROUP
     dma = pltpu.SemaphoreType.DMA
     vmem = pl.BlockSpec(memory_space=pltpu.VMEM)
-    grad_queries, grad = pl.pallas_call(
+    grad_queries, grad, square = pl.pallas_call(
         functools.partial(kernel, reps, shards, per_target),
         out_shape=(
             jax.ShapeDtypeStruct((tokens, width), F32),
             jax.ShapeDtypeStruct((uniq, width), F32),
+            jax.ShapeDtypeStruct((uniq, 128), F32),
         ),
-        in_specs=[vmem] * 3,
-        out_specs=(vmem, vmem),
+        in_specs=[vmem] * 4,
+        out_specs=(pl.BlockSpec(memory_space=pl.ANY), pl.BlockSpec(memory_space=pl.ANY), vmem),
         scratch_shapes=[
+            pltpu.VMEM((QUAD, depth, 1, 128), jnp.int32),
+            pltpu.VMEM((tokens, width), F32),
+            dma((CHUNKS + 1,)),
             pltpu.VMEM((shards, 1, 128), jnp.int32),
             pltpu.VMEM((members, depth, 1, 128), jnp.int32),
             pltpu.VMEM((bands, uniq, columns), BF16),
@@ -477,7 +580,7 @@
             pltpu.VMEM((CHUNKS, shards, per_peer, span), BF16),
             pltpu.VMEM((CHUNKS, reps, uniq // reps, span), F32),
             pltpu.VMEM((CHUNKS, reps, uniq // reps, span), F32),
-            pltpu.VMEM((CHUNKS, reps, uniq // reps, span), F32),
+            pltpu.VMEM((CHUNKS, uniq, span), F32),
             dma,
             dma,
             dma,
@@ -492,6 +595,10 @@
             dma,
             dma((CHUNKS,)),
             dma,
+            dma((CHUNKS,)),
+            pltpu.VMEM((CHUNKS, reps // LOW, uniq // reps, span), F32),
+            dma,
+            dma((CHUNKS,)),
             dma((CHUNKS,)),
         ],
         compiler_params=pltpu.CompilerParams(
@@ -502,8 +609,10 @@
             bytes_accessed=width * (6 * tokens + 8 * uniq),
             transcendentals=tokens * cands,
         ),
-    )(ids, queries, table_rows)
-    new_rows, new_first, new_second = adam_rows(table_rows, first_moment, second_moment, grad)
+    )(target_ids.T, negative_ids.T, queries, table_rows)
+    new_rows, new_first, new_second = adam_rows(
+        table_rows, first_moment, second_moment, grad, square
+    )
     return (new_rows, new_first, new_second, grad_queries)
 
 

time: 144 us -> 137 us (0.951); the launches traced: 142 us -> 137 us
  Pallas kernels: 135 us -> 130 us
    pallas_call x1, Pallas kernels: 135 us -> 130 us  [per_device(): pl.pallas_call(functools.partial(kernel, reps, shards, per_target), out_s...]
    reduce_sum x1 -> x0, other arithmetic: 1.46 us -> none  [adam_rows(): new_second = 0.999 * second + 0.001 * jnp.mean(grad * grad, axis=-1)]
where the time goes in v3:
time: 137 us
  Pallas kernels  130 us (95%)
  other arithmetic  4.61 us (3%)
    pallas_call x1, Pallas kernels, per_device(): pl.pallas_call(functools.partial(kernel, reps, shards, per_target), out_s...  130 us
    sub x1, other arithmetic, adam_rows(): new_rows = rows - 0.01 * new_first / (jnp.sqrt(new_second)[:, None] + 1e-08)  2.94 us

profile of v3, /device:TPU:6, one launch (start us, length us, event | category | flops | bytes accessed | tf_op | source)
XLA Modules:
  0.0 136.9 jit_solution(7367074785783250731)
XLA Ops:
  0.6 0.0 copy-start.3
  0.6 0.0 copy-start.1
  0.7 0.0 copy-start.2
  0.7 130.5 %shard_map.93 = (f32[768,512]{1,0:T(8,128)}, f32[512,512]{1,0:T(8,128)}, f32[512,128]{1,0:T(8,128)}) custom-call(s32[16,48]{1,0:T(8,128)} %bitcast.2, s32[16,48]{1,0:T(8,128)} %bitcast.3, bf16[768,512]{1,0:T(8,128)(2,1)} %q_ref.1, f32[512,512]{1,0:T(8,128)} %table_ref.1), custom_call_target="tpu_custom_call" | custom-call | flops 5234491392 | bytes 4456448 | tf_op jit(solution)/shard_map/pallas_call | solution.py:551
  131.2 1.1 multiply_reduce_fusion
  132.3 0.0 copy-done.3
  132.3 0.6 sqrt_add_fusion
  132.9 0.0 copy-done.1
  132.9 0.0 copy-done.2
  132.9 0.0 copy-start
  132.9 2.9 %divide_subtract_fusion = (f32[512,512]{1,0:T(8,128)}, f32[512,512]{1,0:T(8,128)}) fusion(f32[512,512]{1,0:T(8,128)S(1)} %copy-done.1, f32[512]{0:T(512)S(1)} %get-tuple-element.12, f32[512,512]{1,0:T(8,128)} %get-tuple-element.7, f32[512,512]{1,0:T(8,128)S(1)} %copy-done.2), kind=kLoop, calls=%fused_computation | loop fusion | flops 1572864 | bytes 5244928 | tf_op jit(solution)/shard_map/sub | solution.py:533
  135.8 0.0 copy-done
  135.8 1.1 copy.11
Async XLA Ops:
  0.6 131.6 %copy-start.3 = (f32[512]{0:T(512)S(1)}, f32[512]{0:T(512)}, u32[]{:S(2)}) copy-start(f32[512]{0:T(512)} %param.11) | copy-start | bytes 6148
  0.6 132.2 %copy-start.1 = (f32[512,512]{1,0:T(8,128)S(1)}, f32[512,512]{1,0:T(8,128)}, u32[]{:S(2)}) copy-start(f32[512,512]{1,0:T(8,128)} %table_ref.1) | copy-start | bytes 3145732
  0.7 132.2 %copy-start.2 = (f32[512,512]{1,0:T(8,128)S(1)}, f32[512,512]{1,0:T(8,128)}, u32[]{:S(2)}) copy-start(f32[512,512]{1,0:T(8,128)} %param.10) | copy-start | bytes 3145732
  132.9 2.9 %copy-start = (f32[768,512]{1,0:T(8,128)S(1)}, f32[768,512]{1,0:T(8,128)}, u32[]{:S(2)}) copy-start(f32[768,512]{1,0:T(8,128)} %get-tuple-element.21) | copy-start | bytes 4718596

commit v4 on v3

--- a/solution.py
+++ b/solution.py
@@ -46,12 +46,10 @@
     negatives_ref,
     q_ref,
     table_ref,
-    gq_out,
-    grad_out,
+    gq_ref,
+    grad_ref,
     square_ref,
     ids_ref,
-    gq_ref,
-    out_sem,
     ids_in,
     ids_plane,
     minus,
@@ -296,7 +294,8 @@
                 {"shard": peer},
             ).start()
 
-    def row_grads(band, carry):
+    def row_grads(turn, carry):
+        band = bands - 1 - turn
         place = iota((band_rows, 1), 0)
         quad = place // (2 * per_peer)
         level = jnp.where(place // per_peer % 2 == 1, z + band, z + depth - band - 1)
@@ -321,7 +320,8 @@
     lax.fori_loop(0, bands, row_grads, 0)
     for chunk in range(1, CHUNKS):
 
-        def later(band, carry):
+        def later(turn, carry):
+            band = bands - 1 - turn
             for entry in range(BAND):
                 send_back(chunk, band, entry)
             return carry
@@ -365,7 +365,6 @@
         return carry
 
     lax.fori_loop(0, tokens // tile, query_grads, 0)
-    pltpu.make_async_copy(gq_ref, gq_out, out_sem.at[CHUNKS]).start()
 
     def reduce_chunk(chunk):
         push(
@@ -461,13 +460,6 @@
             across,
         ).start()
 
-    def to_grad(chunk):
-        return pltpu.make_async_copy(
-            gathered.at[chunk],
-            grad_out.at[:, pl.ds(chunk * span, span)],
-            out_sem.at[chunk],
-        )
-
     def finish_chunk(chunk):
         if chunk < STAGED:
             push(
@@ -486,8 +478,8 @@
                 full_recv.at[chunk],
                 up,
             ).wait_recv()
-        to_grad(chunk).start()
         part = gathered[chunk]
+        grad_ref[:, chunk * span : (chunk + 1) * span] = part
         return jnp.sum(part * part, axis=-1, keepdims=True)
 
     for chunk in range(CHUNKS):
@@ -523,15 +515,41 @@
             push(
                 gathered.at[chunk, half_rows], gathered.at[chunk, half_rows], cross_send, ids_recv, up
             ).wait_send()
-        to_grad(chunk).wait()
-    pltpu.make_async_copy(gq_ref, gq_out, out_sem.at[CHUNKS]).wait()
+
+
+def adam_kernel(rows_ref, first_ref, second_ref, grad_ref, square_ref, new_rows, new_first, new_second):
+    lanes = square_ref.shape[1]
+    width = grad_ref.shape[1]
+    at = pl.program_id(0)
+    second = jnp.transpose(jnp.broadcast_to(second_ref[at], (lanes, lanes)))
+    second = 0.999 * second + 0.001 * (square_ref[...] / width)
+    new_second[at] = jnp.transpose(second)[0:1]
+    root = jnp.sqrt(second) + 1e-08
+    for k in range(width // lanes):
+        part = slice(k * lanes, (k + 1) * lanes)
+        first = 0.9 * first_ref[:, part] + 0.1 * grad_ref[:, part]
+        new_first[:, part] = first
+        new_rows[:, part] = rows_ref[:, part] - 0.01 * first / root
 
 
 def adam_rows(rows, first, second, grad, square):
-    new_first = 0.9 * first + 0.1 * grad
-    new_second = 0.999 * second + 0.001 * (square[:, 0] / grad.shape[1])
-    new_rows = rows - 0.01 * new_first / (jnp.sqrt(new_second)[:, None] + 1e-08)
-    return (new_rows, new_first, new_second)
+    uniq, width = rows.shape
+    lanes = square.shape[1]
+    blocks = uniq // lanes
+    block = pl.BlockSpec((lanes, width), lambda i: (i, 0))
+    line = pl.BlockSpec((blocks, 1, lanes), lambda i: (0, 0, 0))
+    table = jax.ShapeDtypeStruct((uniq, width), F32)
+    new_rows, new_first, new_second = pl.pallas_call(
+        adam_kernel,
+        grid=(blocks,),
+        out_shape=(table, table, jax.ShapeDtypeStruct((blocks, 1, lanes), F32)),
+        in_specs=[block, block, line, block, pl.BlockSpec((lanes, lanes), lambda i: (i, 0))],
+        out_specs=(block, block, line),
+        cost_estimate=pl.CostEstimate(
+            flops=8 * uniq * width, bytes_accessed=20 * uniq * width, transcendentals=uniq
+        ),
+    )(rows, first, second.reshape(blocks, 1, lanes), grad, square)
+    return (new_rows, new_first, new_second.reshape(uniq))
 
 
 def per_device(reps, shards, queries, target_ids, negative_ids, table_rows, first_moment, second_moment):
@@ -556,11 +574,9 @@
             jax.ShapeDtypeStruct((uniq, 128), F32),
         ),
         in_specs=[vmem] * 4,
-        out_specs=(pl.BlockSpec(memory_space=pl.ANY), pl.BlockSpec(memory_space=pl.ANY), vmem),
+        out_specs=(vmem, vmem, vmem),
         scratch_shapes=[
             pltpu.VMEM((QUAD, depth, 1, 128), jnp.int32),
-            pltpu.VMEM((tokens, width), F32),
-            dma((CHUNKS + 1,)),
             pltpu.VMEM((shards, 1, 128), jnp.int32),
             pltpu.VMEM((members, depth, 1, 128), jnp.int32),
             pltpu.VMEM((bands, uniq, columns), BF16),

time: 137 us -> 135 us (0.985); the launches traced: 137 us -> 133 us
  other arithmetic: 4.61 us -> 0 us
    pallas_call x0 -> x1, Pallas kernels: none -> 4.14 us  [adam_rows(): pl.pallas_call(adam_kernel, grid=(blocks,), out_shape=(table, table, jax....]
    pallas_call x1, Pallas kernels: 130 us -> 127 us  [per_device(): pl.pallas_call(functools.partial(kernel, reps, shards, per_target), out_s...]
    sub x1 -> x0, other arithmetic: 2.94 us -> none  [adam_rows(): new_rows = rows - 0.01 * new_first / (jnp.sqrt(new_second)[:, None] + 1e-08)]
where the time goes in v4:
time: 135 us; the launch traced here: 133 us
  Pallas kernels  131 us (97%)
    pallas_call x1, Pallas kernels, per_device(): pl.pallas_call(functools.partial(kernel, reps, shards, per_target), out_s...  127 us
    pallas_call x1, Pallas kernels, adam_rows(): pl.pallas_call(adam_kernel, grid=(blocks,), out_shape=(table, table, jax....  4.14 us

profile of v4, /device:TPU:6, one launch (start us, length us, event | category | flops | bytes accessed | tf_op | source)
XLA Modules:
  0.0 132.5 jit_solution(288416242027508521)
XLA Ops:
  0.6 126.6 %shard_map.93 = (f32[768,512]{1,0:T(8,128)}, f32[512,512]{1,0:T(8,128)}, f32[512,128]{1,0:T(8,128)}) custom-call(s32[16,48]{1,0:T(8,128)} %bitcast.5, s32[16,48]{1,0:T(8,128)} %bitcast.6, bf16[768,512]{1,0:T(8,128)(2,1)} %q_ref.1, f32[512,512]{1,0:T(8,128)} %rows_ref.1), custom_call_target="tpu_custom_call" | custom-call | flops 5234491392 | bytes 4456448 | tf_op jit(solution)/shard_map/pallas_call | solution.py:569
  127.2 0.0 copy-start
  127.2 4.1 %shard_map.94 = (f32[512,512]{1,0:T(8,128)}, f32[512,512]{1,0:T(8,128)}, f32[4,1,128]{2,1,0:T(1,128)}) custom-call(f32[512,512]{1,0:T(8,128)} %rows_ref.1, f32[512,512]{1,0:T(8,128)} %first_ref.1, f32[4,1,128]{2,1,0:T(1,128)} %bitcast.4, f32[512,512]{1,0:T(8,128)} %get-tuple-element.10.grad_ref, f32[512,128]{1,0:T(8,128)} %get-tuple-element.11.square_ref), custom_call_target="tpu_custom_call" | custom-call | flops 2097152 | bytes 5242880 | tf_op jit(solution)/shard_map/pallas_call | solution.py:542
  131.4 0.0 copy-done
  131.4 1.1 copy.11
Async XLA Ops:
  127.2 4.2 %copy-start = (f32[768,512]{1,0:T(8,128)S(1)}, f32[768,512]{1,0:T(8,128)}, u32[]{:S(2)}) copy-start(f32[768,512]{1,0:T(8,128)} %get-tuple-element.23) | copy-start | bytes 4718596

commit v5 on v4

--- a/solution.py
+++ b/solution.py
@@ -12,6 +12,7 @@
 CHUNKS = 4
 PIECES = 2
 STAGED = 3
+STEPS = 2
 LOW = 2
 CORES = 2
 QUAD = 4
@@ -518,33 +519,37 @@
 
 
 def adam_kernel(rows_ref, first_ref, second_ref, grad_ref, square_ref, new_rows, new_first, new_second):
-    lanes = square_ref.shape[1]
+    rows, lanes = square_ref.shape
     width = grad_ref.shape[1]
-    at = pl.program_id(0)
-    second = jnp.transpose(jnp.broadcast_to(second_ref[at], (lanes, lanes)))
-    second = 0.999 * second + 0.001 * (square_ref[...] / width)
-    new_second[at] = jnp.transpose(second)[0:1]
-    root = jnp.sqrt(second) + 1e-08
-    for k in range(width // lanes):
-        part = slice(k * lanes, (k + 1) * lanes)
-        first = 0.9 * first_ref[:, part] + 0.1 * grad_ref[:, part]
-        new_first[:, part] = first
-        new_rows[:, part] = rows_ref[:, part] - 0.01 * first / root
+    for block in range(rows // lanes):
+        at = pl.program_id(0) * (rows // lanes) + block
+        here = slice(block * lanes, (block + 1) * lanes)
+        second = jnp.transpose(jnp.broadcast_to(second_ref[at], (lanes, lanes)))
+        second = 0.999 * second + 0.001 * (square_ref[here] / width)
+        new_second[at] = jnp.transpose(second)[0:1]
+        root = jnp.sqrt(second) + 1e-08
+        for k in range(width // lanes):
+            part = slice(k * lanes, (k + 1) * lanes)
+            first = 0.9 * first_ref[here, part] + 0.1 * grad_ref[here, part]
+            new_first[here, part] = first
+            new_rows[here, part] = rows_ref[here, part] - 0.01 * first / root
 
 
 def adam_rows(rows, first, second, grad, square):
     uniq, width = rows.shape
     lanes = square.shape[1]
     blocks = uniq // lanes
-    block = pl.BlockSpec((lanes, width), lambda i: (i, 0))
+    tall = uniq // STEPS
+    block = pl.BlockSpec((tall, width), lambda i: (i, 0))
     line = pl.BlockSpec((blocks, 1, lanes), lambda i: (0, 0, 0))
     table = jax.ShapeDtypeStruct((uniq, width), F32)
     new_rows, new_first, new_second = pl.pallas_call(
         adam_kernel,
-        grid=(blocks,),
+        grid=(STEPS,),
         out_shape=(table, table, jax.ShapeDtypeStruct((blocks, 1, lanes), F32)),
-        in_specs=[block, block, line, block, pl.BlockSpec((lanes, lanes), lambda i: (i, 0))],
+        in_specs=[block, block, line, block, pl.BlockSpec((tall, lanes), lambda i: (i, 0))],
         out_specs=(block, block, line),
+        compiler_params=pltpu.CompilerParams(vmem_limit_bytes=32 * 1024 * 1024),
         cost_estimate=pl.CostEstimate(
             flops=8 * uniq * width, bytes_accessed=20 * uniq * width, transcendentals=uniq
         ),

time: 135 us -> 137 us (1.015)
  the two profiles are of different devices: /device:TPU:6 before, /device:TPU:70 now
where the time goes in v5:
time: 137 us
  Pallas kernels  133 us (97%)
  local copies, waits for them, and re-layouts  3.82 us (3%)
    pallas_call x1, Pallas kernels, per_device(): pl.pallas_call(functools.partial(kernel, reps, shards, per_target), out_s...  131 us
    unnamed x13, local copies, waits for them, and re-layouts  3.82 us

profile of v5, /device:TPU:70, one launch (start us, length us, event | category | flops | bytes accessed | tf_op | source)
XLA Modules:
  0.0 137.2 jit_solution(5785471184119470610)
XLA Ops:
  0.6 0.0 copy-start
  0.6 0.0 copy-start.1
  0.7 0.0 copy-start.4
  0.7 131.1 %shard_map.93 = (f32[768,512]{1,0:T(8,128)}, f32[512,512]{1,0:T(8,128)}, f32[512,128]{1,0:T(8,128)}) custom-call(s32[16,48]{1,0:T(8,128)} %bitcast.5, s32[16,48]{1,0:T(8,128)} %bitcast.6, bf16[768,512]{1,0:T(8,128)(2,1)} %q_ref.1, f32[512,512]{1,0:T(8,128)} %rows_ref.1), custom_call_target="tpu_custom_call" | custom-call | flops 5234491392 | bytes 4456448 | tf_op jit(solution)/shard_map/pallas_call | solution.py:574
  131.8 0.0 copy-done
  131.8 0.0 copy-done.1
  131.8 0.0 copy-done.4
  131.8 0.0 copy-start.2
  131.8 1.2 copy-done.2
  133.0 0.0 copy-start.3
  133.0 0.9 copy-done.3
  134.0 0.0 copy-start.5
  134.0 1.5 %shard_map.94 = (f32[512,512]{1,0:T(8,128)}, f32[512,512]{1,0:T(8,128)}, f32[4,1,128]{2,1,0:T(1,128)}) custom-call(f32[512,512]{1,0:T(8,128)S(1)} %copy-done, f32[512,512]{1,0:T(8,128)S(1)} %copy-done.1, f32[4,1,128]{2,1,0:T(1,128)S(1)} %bitcast.4, f32[512,512]{1,0:T(8,128)S(1)} %copy-done.2, f32[512,128]{1,0:T(8,128)S(1)} %copy-done.3), custom_call_target="tpu_custom_call" | custom-call | flops 2097152 | bytes 5242880 | tf_op jit(solution)/shard_map/pallas_call | solution.py:546
  135.5 0.5 copy-done.5
  136.0 1.1 copy.11
Async XLA Ops:
  0.6 131.2 %copy-start = (f32[512,512]{1,0:T(8,128)S(1)}, f32[512,512]{1,0:T(8,128)}, u32[]{:S(2)}) copy-start(f32[512,512]{1,0:T(8,128)} %rows_ref.1) | copy-start | bytes 3145732
  0.6 131.2 %copy-start.1 = (f32[512,512]{1,0:T(8,128)S(1)}, f32[512,512]{1,0:T(8,128)}, u32[]{:S(2)}) copy-start(f32[512,512]{1,0:T(8,128)} %first_ref.1) | copy-start | bytes 3145732
  0.7 131.2 %copy-start.4 = (f32[512]{0:T(512)S(1)}, f32[512]{0:T(512)}, u32[]{:S(2)}) copy-start(f32[512]{0:T(512)} %param.11) | copy-start | bytes 6148
  131.8 1.2 copy-start.2
  133.0 0.9 copy-start.3
  134.0 2.0 %copy-start.5 = (f32[768,512]{1,0:T(8,128)S(1)}, f32[768,512]{1,0:T(8,128)}, u32[]{:S(2)}) copy-start(f32[768,512]{1,0:T(8,128)} %get-tuple-element.23) | copy-start | bytes 4718596
